TPU v7x, 32 devices: a whole 2x2x4 slice. The times are simulated.
32 devices in a mesh: grp: 2 (over x), row: 16 (over z, y, core).
Axes of the slice: x: 2, y: 2, z: 4, core: 2. Of those that a mesh axis runs over, the one named last changes fastest.
Arguments:
- vis_values: bfloat16 [2, 32768], P(None, ('grp', 'row')), parts along dimension 1, may hold values from -6 to 6
- tile_row: int32 [32768], P(('grp', 'row')), parts along dimension 0, may hold values from 0 to 15, as said below
- tile_col: int32 [32768], P(('grp', 'row')), parts along dimension 0, may hold values from 0 to 1
- row_offset: int32 [32768], P(('grp', 'row')), parts along dimension 0, may hold values from 0 to 127
- col_offset: int32 [32768], P(('grp', 'row')), parts along dimension 0, may hold values from 0 to 127
- plane: int32 [32768], P(('grp', 'row')), parts along dimension 0, may hold values from 0 to 7
- plane_w: float32 [16], P('grp'), parts along dimension 0, may hold values from -1000 to 1000
Outputs:
- dirty: float32 [512, 1024], P(('grp', 'row')), parts along dimension 0
There are 2 independent parts, one for each index of `grp`. A program takes and returns all parts, laid end to end along the dimension named above; each array names one. Nothing has to cross between parts.
Inputs may be any that keep to these rules, and one draw needn't show every extreme that they name: `tile_row`: in each device's block of 1024 visibilities no tile row is named more than 256 times; one tile row, the same for every device of a part, is named exactly 256 times in every block.
All inputs are finite; a program needn't handle non-finite values.
Results may differ from a plain program's by a relative error of at most 0.006.
Values may be sent and summed in bfloat16 or wider, within the bound.
A program may use at most 128 MiB of HBM per device.

v0:
```python
import functools
import math

import jax
import jax.numpy as jnp
from jax import lax
from jax.experimental import pallas as pl
from jax.experimental.pallas import tpu as pltpu
from jax.sharding import PartitionSpec as P

G = 32768
W = 8
TILE = 128
L_OUT = 1024
M_DEV = 16
U_START = 8192
V_START = 8192
V_WIN = 256
F32 = jnp.float32
BF16 = jnp.bfloat16
I32 = jnp.int32
NT = (((1,), (1,)), ((), ()))
SINE = [(-1) ** k * (2.0 * math.pi) ** (2 * k + 1) / math.factorial(2 * k + 1) for k in range(6)]


def quarter_sine(s):
    square = s * s
    total = jnp.full_like(s, SINE[5])
    for k in range(4, -1, -1):
        total = total * square + SINE[k]
    return total * s


def cos_turns(t):
    return quarter_sine(0.25 - jnp.abs(t))


def sin_turns(t):
    return quarter_sine(jnp.abs(jnp.abs(t - 0.25) - 0.5) - 0.25)


def wrap(turns):
    return (((turns + G // 2) & (G - 1)) - G // 2).astype(F32) * (1.0 / G)


def iota(shape, axis):
    return lax.broadcasted_iota(I32, shape, axis)


def pixel(index, step):
    return ((index * step) & (G - 1)) - G // 2


def taper(spread):
    return jnp.where(jnp.abs(spread) <= 4.0, jnp.exp(spread * spread * -0.125), 0.0)


def kernel(
    devices, cap, group, width, per_device,
    data_ref, w_ref, out_ref,
    key_s, send1, recv1, a_s, b_s, grid_s, tv_s, send2, recv2, tab_s, e1c, e1s, e2c, e2s, scr_c, scr_s,
    ss1, rs1, ss2, rs2,
):
    me = lax.axis_index("row")
    blocks = devices // group
    m_step = G // (M_DEV * devices) + 1
    l_step = G // L_OUT + 1
    barrier = pltpu.get_barrier_semaphore()

    def greet(i, carry):
        pl.semaphore_signal(
            barrier, inc=1, device_id={"row": lax.rem(me + i, devices)},
            device_id_type=pl.DeviceIdType.MESH,
        )
        return carry

    lax.fori_loop(1, devices, greet, 0)

    def copy1(i):
        peer = lax.rem(me + i, devices)
        return pltpu.make_async_remote_copy(
            src_ref=send1.at[peer], dst_ref=recv1.at[me], send_sem=ss1.at[i], recv_sem=rs1.at[i],
            device_id={"row": peer}, device_id_type=pl.DeviceIdType.MESH,
        )

    def arrive1(i):
        source = lax.rem(me - i + devices, devices)
        return pltpu.make_async_remote_copy(
            src_ref=send1.at[source], dst_ref=recv1.at[source], send_sem=ss1.at[i], recv_sem=rs1.at[i],
            device_id={"row": source}, device_id_type=pl.DeviceIdType.MESH,
        )

    def copy2(i):
        peer = lax.rem(me + i, devices)
        return pltpu.make_async_remote_copy(
            src_ref=send2.at[peer], dst_ref=recv2.at[me], send_sem=ss2.at[i], recv_sem=rs2.at[i],
            device_id={"row": peer}, device_id_type=pl.DeviceIdType.MESH,
        )

    def arrive2(i):
        source = lax.rem(me - i + devices, devices)
        return pltpu.make_async_remote_copy(
            src_ref=send2.at[source], dst_ref=recv2.at[source], send_sem=ss2.at[i], recv_sem=rs2.at[i],
            device_id={"row": source}, device_id_type=pl.DeviceIdType.MESH,
        )

    with jax.named_scope("pack"):
        data = data_ref[...]
        member = jnp.where(data[6:7, :] == iota((devices, per_device), 0).astype(F32), 1.0, 0.0)
        parts = [member[:, c * 128 : (c + 1) * 128] for c in range(per_device // 128)]
        below = jnp.where(iota((128, 128), 0) < iota((128, 128), 1), 1.0, 0.0).astype(BF16)
        ranks = jnp.dot(jnp.concatenate(parts, axis=0).astype(BF16), below, preferred_element_type=F32)
        before = jnp.zeros((devices, 1), F32) + lax.rem(me, group).astype(F32) * cap
        for c, part in enumerate(parts):
            rank = ranks[c * devices : (c + 1) * devices] + before
            key_s[:, c * 128 : (c + 1) * 128] = jnp.where(part > 0.0, rank, -1.0)
            before = before + jnp.sum(part, axis=1, keepdims=True)
        low = data.astype(BF16)

        def packed(d):
            slot = iota((width, per_device), 0).astype(F32)
            hot = jnp.where(slot == key_s[pl.ds(d, 1), :], 1.0, 0.0).astype(BF16)
            return lax.dot_general(low, hot, NT, preferred_element_type=F32)

        pl.semaphore_wait(barrier, devices - 1)

        def send_block(i, carry):
            d = lax.rem(me + i, devices)
            send1[d] = packed(d)
            copy1(i).start()
            return carry

        lax.fori_loop(1, devices, send_block, 0)
        recv1[me] = packed(me)

    with jax.named_scope("tables"):
        rows = 2 * M_DEV * devices
        tile_rows = 256

        def table_v(k, carry):
            row = iota((tile_rows, V_WIN), 0) + k * tile_rows
            owner = row >> 5
            part = (row >> 4) & 1
            om = pixel((row & 15) * devices + owner, m_step)
            turns = (iota((tile_rows, V_WIN), 1) + V_START) * om
            at = pl.ds(pl.multiple_of(k * tile_rows, tile_rows), tile_rows)
            tv_s[at, :V_WIN] = cos_turns(wrap(turns - part * (G // 4))).astype(BF16)
            tv_s[at, V_WIN:] = cos_turns(wrap(turns + (1 - part) * (G // 4))).astype(BF16)
            return carry

        lax.fori_loop(0, rows // tile_rows, table_v, 0)
        ol = pixel(iota((TILE, L_OUT), 1), l_step)
        turn2 = wrap(iota((TILE, L_OUT), 0) * ol)
        e2c[...] = cos_turns(turn2)
        e2s[...] = sin_turns(turn2)
        ol1 = pixel(iota((devices, L_OUT), 1), l_step)
        turn1 = wrap((iota((devices, L_OUT), 0) * TILE + U_START) * ol1)
        e1c[...] = cos_turns(turn1)
        e1s[...] = sin_turns(turn1)

    def wait1(i, carry):
        arrive1(i).wait_recv()
        return carry

    lax.fori_loop(1, devices, wait1, 0)

    with jax.named_scope("spread"):

        def spread(k, carry):
            block = recv1[k * group]
            for j in range(1, group):
                block = block + recv1[k * group + j]
            at = pl.ds(pl.multiple_of(k * width, width), width)
            down = iota((TILE, width), 0).astype(F32)
            rows_k = taper(down - block[3:4, :]).astype(BF16)
            for p in range(W):
                mask = jnp.where(block[2:3, :] == p + 1.0, 1.0, 0.0).astype(BF16)
                b_s[p * TILE : (p + 1) * TILE, at] = rows_k * mask
            cols_k = taper(down - block[5:6, :])
            for e in range(2):
                for h in range(2):
                    value = jnp.where(block[4:5, :] == float(h), block[e : e + 1, :], 0.0)
                    first = e * V_WIN + h * TILE
                    a_s[first : first + TILE, at] = (cols_k * value).astype(BF16)
            return carry

        lax.fori_loop(0, blocks, spread, 0)

    with jax.named_scope("gridding"):

        def grid_tile(j, carry):
            at = pl.ds(pl.multiple_of(j * 256, 256), 256)
            grid_s[:, at] = lax.dot_general(a_s[...], b_s[at, :], NT, preferred_element_type=F32).astype(BF16)
            return carry

        lax.fori_loop(0, W * TILE // 256, grid_tile, 0)

    with jax.named_scope("columns"):
        per_step = 8

        def columns(k, carry):
            at = pl.ds(pl.multiple_of(k * 32 * per_step, 32 * per_step), 32 * per_step)
            block = jnp.dot(tv_s[at, :], grid_s[...], preferred_element_type=F32).astype(BF16)
            for j in range(per_step):
                send2[k * per_step + j] = block[j * 32 : (j + 1) * 32]
            return carry

        lax.fori_loop(0, devices // per_step, columns, 0)

        def start2(i, carry):
            copy2(i).start()
            return carry

        lax.fori_loop(1, devices, start2, 0)
        recv2[me] = send2[me]

    with jax.named_scope("row_table"):

        def table_u(s, carry):
            at = pl.ds(pl.multiple_of(s * TILE, TILE), TILE)
            c1, s1 = e1c[pl.ds(s, 1), :], e1s[pl.ds(s, 1), :]
            c2, s2 = e2c[...], e2s[...]
            tab_s[at, :L_OUT] = (c1 * c2 - s1 * s2).astype(BF16)
            tab_s[at, L_OUT:] = (s1 * c2 + c1 * s2).astype(BF16)
            return carry

        lax.fori_loop(0, devices, table_u, 0)

    with jax.named_scope("screen"):
        scale = 1.0 / math.sqrt(per_device * devices)
        y = pixel(iota((M_DEV, L_OUT), 0) * devices + me, m_step).astype(F32) * (1.0 / G)
        x = pixel(iota((M_DEV, L_OUT), 1), l_step).astype(F32) * (1.0 / G)
        q = x * x + y * y
        lowered = q / (1.0 + jnp.sqrt(1.0 - q))
        for p in range(W):
            turns = lowered * -w_ref[p]
            turns = turns - jnp.floor(turns + 0.5)
            scr_c[p] = cos_turns(turns) * scale
            scr_s[p] = sin_turns(turns) * scale

    def wait2(i, carry):
        arrive2(i).wait_recv()
        return carry

    lax.fori_loop(1, devices, wait2, 0)

    with jax.named_scope("rows"):

        depth = min(TILE * devices, b_s.shape[1])
        turns_k = TILE * devices // depth
        for h in range(turns_k):

            def regroup(s, carry):
                at = pl.ds(pl.multiple_of(s * TILE, TILE), TILE)
                for p in range(W):
                    first = h * 32 * W + p * 32
                    b_s[first : first + 32, at] = recv2[s + h * (depth // TILE), :, p * TILE : (p + 1) * TILE]
                return carry

            lax.fori_loop(0, depth // TILE, regroup, 0)

        def rows_by(at):
            total = None
            for h in range(turns_k):
                left = b_s[h * 32 * W : (h + 1) * 32 * W, :depth]
                right = tab_s[h * depth : (h + 1) * depth, at]
                part = jnp.dot(left, right, preferred_element_type=F32)
                total = part if total is None else total + part
            return total

        def image(k, carry):
            at = pl.ds(pl.multiple_of(k * 256, 256), 256)
            also = pl.ds(pl.multiple_of(k * 256 + L_OUT, 256), 256)
            by_cos = rows_by(at)
            by_sin = rows_by(also)
            total = jnp.zeros((M_DEV, 256), F32)
            for p in range(W):
                r0, r1, r2 = p * 32, p * 32 + 16, p * 32 + 32
                real = by_cos[r0:r1] - by_sin[r1:r2]
                imag = by_sin[r0:r1] + by_cos[r1:r2]
                total = total + scr_c[p, :, at] * real - scr_s[p, :, at] * imag
            out_ref[:, at] = total
            return carry

        lax.fori_loop(0, L_OUT // 256, image, 0)

    def drain(i, carry):
        copy1(i).wait_send()
        copy2(i).wait_send()
        return carry

    lax.fori_loop(1, devices, drain, 0)


def on_device(vis_values, tile_row, tile_col, row_offset, col_offset, plane, plane_w):
    devices = lax.axis_size("row")
    per_device = vis_values.shape[1]
    cap = 4 * per_device // devices
    group = max(1, 128 // cap)
    width = cap * group
    slots = width * (devices // group)
    ints = jnp.stack([plane + 1, row_offset, tile_col, col_offset, tile_row, jnp.zeros_like(plane)])
    data = jnp.concatenate([vis_values.astype(F32), ints.astype(F32)], axis=0)
    vmem = pl.BlockSpec(memory_space=pltpu.VMEM)
    return pl.pallas_call(
        functools.partial(kernel, devices, cap, group, width, per_device),
        out_shape=jax.ShapeDtypeStruct((M_DEV, L_OUT), F32),
        in_specs=[vmem, pl.BlockSpec(memory_space=pltpu.SMEM)],
        out_specs=vmem,
        scratch_shapes=[
            pltpu.VMEM((devices, per_device), F32),
            pltpu.VMEM((devices, 8, width), F32),
            pltpu.VMEM((devices, 8, width), F32),
            pltpu.VMEM((2 * V_WIN, slots), BF16),
            pltpu.VMEM((W * TILE, slots), BF16),
            pltpu.VMEM((2 * V_WIN, W * TILE), BF16),
            pltpu.VMEM((2 * M_DEV * devices, 2 * V_WIN), BF16),
            pltpu.VMEM((devices, 2 * M_DEV, W * TILE), BF16),
            pltpu.VMEM((devices, 2 * M_DEV, W * TILE), BF16),
            pltpu.VMEM((TILE * devices, 2 * L_OUT), BF16),
            pltpu.VMEM((devices, L_OUT), F32),
            pltpu.VMEM((devices, L_OUT), F32),
            pltpu.VMEM((TILE, L_OUT), F32),
            pltpu.VMEM((TILE, L_OUT), F32),
            pltpu.VMEM((W, M_DEV, L_OUT), F32),
            pltpu.VMEM((W, M_DEV, L_OUT), F32),
            pltpu.SemaphoreType.DMA((devices,)),
            pltpu.SemaphoreType.DMA((devices,)),
            pltpu.SemaphoreType.DMA((devices,)),
            pltpu.SemaphoreType.DMA((devices,)),
        ],
        compiler_params=pltpu.CompilerParams(
            collective_id=0, has_side_effects=True, vmem_limit_bytes=(32 if devices <= 16 else 62) * 2**20
        ),
    )(data, plane_w)


def solution(mesh):
    vector = P(("grp", "row"))
    in_specs = (P(None, ("grp", "row")), vector, vector, vector, vector, vector, P("grp"))
    return jax.shard_map(
        on_device, mesh=mesh, in_specs=in_specs, out_specs=P(("grp", "row"), None), check_vma=False
    )
```

profile of v0, /device:TPU:13, one launch (start us, length us, event | category | flops | bytes accessed | tf_op | source)
XLA Modules:
  0.0 51.3 jit_solution(15608501842863960832)
XLA Ops:
  0.0 0.0 copy-start.6
  0.0 0.7 %copy-done.6 = s32[1024]{0:T(1024)S(1)} copy-done((s32[1024]{0:T(1024)S(1)}, s32[1024]{0:T(1024)}, u32[]{:S(2)}) %copy-start.6) | copy-done | bytes 4120
  0.7 0.0 copy-start.5
  0.7 0.7 %copy-done.5 = bf16[2,1024]{1,0:T(2,128)(2,1)S(1)} copy-done((bf16[2,1024]{1,0:T(2,128)(2,1)S(1)}, bf16[2,1024]{1,0:T(2,128)(2,1)}, u32[]{:S(2)}) %copy-start.5) | copy-done | bytes 4120
  1.4 0.0 copy-start.2
  1.4 0.0 copy-start.3
  1.4 0.0 copy-start.4
  1.4 0.0 copy-start.1
  1.4 0.6 %copy-done.2 = s32[1024]{0:T(1024)S(1)} copy-done((s32[1024]{0:T(1024)S(1)}, s32[1024]{0:T(1024)}, u32[]{:S(2)}) %copy-start.2) | copy-done | bytes 4120
  2.1 0.0 copy-done.3
  2.1 0.0 copy-done.4
  2.1 0.0 copy-done.1
  2.2 0.0 copy-start
  2.2 0.6 %copy-done = f32[8]{0:T(128)S(1)} copy-done((f32[8]{0:T(128)S(1)}, f32[8]{0:T(128)}, u32[]{:S(2)}) %copy-start) | copy-done | bytes 56
  2.8 47.8 %shard_map.73 = f32[16,1024]{1,0:T(8,128)S(1)} custom-call(f32[8,1024]{1,0:T(8,128)S(1)} %pad_maximum_fusion.data_ref, f32[8]{0:T(128)S(1)} %copy-done), custom_call_target="tpu_custom_call" | custom-call | tf_op jit(solution)/shard_map/pallas_call | solution.py:305
  50.6 0.6 %copy.9 = f32[16,1024]{1,0:T(8,128)} copy(f32[16,1024]{1,0:T(8,128)S(1)} %shard_map.73) | data formatting | bytes 131072
  (6 shorter events, 0.1 us)
Async XLA Ops:
  0.0 0.7 %copy-start.6 = (s32[1024]{0:T(1024)S(1)}, s32[1024]{0:T(1024)}, u32[]{:S(2)}) copy-start(s32[1024]{0:T(1024)} %param.12) | copy-start | bytes 12292
  0.7 0.7 %copy-start.5 = (bf16[2,1024]{1,0:T(2,128)(2,1)S(1)}, bf16[2,1024]{1,0:T(2,128)(2,1)}, u32[]{:S(2)}) copy-start(bf16[2,1024]{1,0:T(2,128)(2,1)} %param.7) | copy-start | bytes 12292
  1.4 0.7 %copy-start.2 = (s32[1024]{0:T(1024)S(1)}, s32[1024]{0:T(1024)}, u32[]{:S(2)}) copy-start(s32[1024]{0:T(1024)} %param.9) | copy-start | bytes 12292
  1.4 0.7 %copy-start.3 = (s32[1024]{0:T(1024)S(1)}, s32[1024]{0:T(1024)}, u32[]{:S(2)}) copy-start(s32[1024]{0:T(1024)} %param.11) | copy-start | bytes 12292
  1.4 0.7 %copy-start.4 = (s32[1024]{0:T(1024)S(1)}, s32[1024]{0:T(1024)}, u32[]{:S(2)}) copy-start(s32[1024]{0:T(1024)} %param.8) | copy-start | bytes 12292
  1.4 0.7 %copy-start.1 = (s32[1024]{0:T(1024)S(1)}, s32[1024]{0:T(1024)}, u32[]{:S(2)}) copy-start(s32[1024]{0:T(1024)} %param.10) | copy-start | bytes 12292
  2.2 0.7 %copy-start = (f32[8]{0:T(128)S(1)}, f32[8]{0:T(128)}, u32[]{:S(2)}) copy-start(f32[8]{0:T(128)} %w_ref.1) | copy-start | bytes 100
where the time goes:
time: 51.6 us; the launch traced here: 51.3 us
  Pallas kernels  47.8 us (93%)
  local copies, waits for them, and re-layouts  3.39 us (7%)
    pallas_call x1, Pallas kernels, on_device(): pl.pallas_call(functools.partial(kernel, devices, cap, group, width, per_...  47.8 us
    unnamed x15, local copies, waits for them, and re-layouts  3.34 us

commit v1 on v0

--- a/solution.py
+++ b/solution.py
@@ -58,8 +58,8 @@
 def kernel(
     devices, cap, group, width, per_device,
     data_ref, w_ref, out_ref,
-    key_s, send1, recv1, a_s, b_s, grid_s, tv_s, send2, recv2, tab_s, e1c, e1s, e2c, e2s, scr_c, scr_s,
-    ss1, rs1, ss2, rs2,
+    key_s, send1, recv1, a_s, b_s, grid_s, tv_s, send2, recv2, tab_s, scr_c, scr_s, own_s, send3, recv3,
+    ss1, rs1, ss2, rs2, ss3, rs3,
 ):
     me = lax.axis_index("row")
     blocks = devices // group
@@ -90,18 +90,27 @@
             device_id={"row": source}, device_id_type=pl.DeviceIdType.MESH,
         )
 
-    def copy2(i):
-        peer = lax.rem(me + i, devices)
+    half = devices // 2
+    core = lax.rem(me, 2)
+    chip = me // 2
+    partner = me + 1 - 2 * core
+    swap = pltpu.make_async_remote_copy(
+        src_ref=send2.at[pl.ds((1 - core) * half, half)], dst_ref=recv2, send_sem=ss2, recv_sem=rs2,
+        device_id={"row": partner}, device_id_type=pl.DeviceIdType.MESH,
+    )
+
+    def copy3(i):
+        there = lax.rem(chip + i, half)
         return pltpu.make_async_remote_copy(
-            src_ref=send2.at[peer], dst_ref=recv2.at[me], send_sem=ss2.at[i], recv_sem=rs2.at[i],
-            device_id={"row": peer}, device_id_type=pl.DeviceIdType.MESH,
-        )
-
-    def arrive2(i):
-        source = lax.rem(me - i + devices, devices)
+            src_ref=send3.at[there], dst_ref=recv3.at[chip], send_sem=ss3.at[i], recv_sem=rs3.at[i],
+            device_id={"row": there * 2 + core}, device_id_type=pl.DeviceIdType.MESH,
+        )
+
+    def arrive3(i):
+        source = lax.rem(chip - i + half, half)
         return pltpu.make_async_remote_copy(
-            src_ref=send2.at[source], dst_ref=recv2.at[source], send_sem=ss2.at[i], recv_sem=rs2.at[i],
-            device_id={"row": source}, device_id_type=pl.DeviceIdType.MESH,
+            src_ref=send3.at[source], dst_ref=recv3.at[source], send_sem=ss3.at[i], recv_sem=rs3.at[i],
+            device_id={"row": source * 2 + core}, device_id_type=pl.DeviceIdType.MESH,
         )
 
     with jax.named_scope("pack"):
@@ -139,7 +148,8 @@
 
         def table_v(k, carry):
             row = iota((tile_rows, V_WIN), 0) + k * tile_rows
-            owner = row >> 5
+            place = row >> 5
+            owner = jnp.where(place < half, place * 2, place * 2 + 1 - devices)
             part = (row >> 4) & 1
             om = pixel((row & 15) * devices + owner, m_step)
             turns = (iota((tile_rows, V_WIN), 1) + V_START) * om
@@ -149,14 +159,29 @@
             return carry
 
         lax.fori_loop(0, rows // tile_rows, table_v, 0)
-        ol = pixel(iota((TILE, L_OUT), 1), l_step)
-        turn2 = wrap(iota((TILE, L_OUT), 0) * ol)
-        e2c[...] = cos_turns(turn2)
-        e2s[...] = sin_turns(turn2)
-        ol1 = pixel(iota((devices, L_OUT), 1), l_step)
-        turn1 = wrap((iota((devices, L_OUT), 0) * TILE + U_START) * ol1)
-        e1c[...] = cos_turns(turn1)
-        e1s[...] = sin_turns(turn1)
+        ol = pixel(iota((2 * TILE, L_OUT), 1), l_step)
+        row_u = iota((2 * TILE, L_OUT), 0)
+        along_u = U_START + jnp.where(row_u < TILE, row_u + me * TILE, row_u - TILE + partner * TILE)
+        turn_u = wrap(along_u * ol)
+        tab_s[:, :L_OUT] = cos_turns(turn_u).astype(BF16)
+        tab_s[:, L_OUT:] = sin_turns(turn_u).astype(BF16)
+
+    with jax.named_scope("screen"):
+
+        def screen(there, carry):
+            row = iota((M_DEV, L_OUT), 0) * devices + there * 2 + core
+            y = pixel(row, m_step).astype(F32) * (1.0 / G)
+            x = pixel(iota((M_DEV, L_OUT), 1), l_step).astype(F32) * (1.0 / G)
+            q = x * x + y * y
+            lowered = q / (1.0 + jnp.sqrt(1.0 - q))
+            for p in range(W):
+                turns = lowered * -w_ref[p]
+                turns = turns - jnp.floor(turns + 0.5)
+                scr_c[there, p] = cos_turns(turns)
+                scr_s[there, p] = sin_turns(turns)
+            return carry
+
+        lax.fori_loop(0, half, screen, 0)
 
     def wait1(i, carry):
         arrive1(i).wait_recv()
@@ -196,100 +221,76 @@
         lax.fori_loop(0, W * TILE // 256, grid_tile, 0)
 
     with jax.named_scope("columns"):
-        per_step = 8
-
-        def columns(k, carry):
-            at = pl.ds(pl.multiple_of(k * 32 * per_step, 32 * per_step), 32 * per_step)
+
+        def columns(k, first):
+            start = first + k * (devices // 4)
+            rows_k = 32 * (devices // 4)
+            at = pl.ds(pl.multiple_of(start * 32, 32), rows_k)
             block = jnp.dot(tv_s[at, :], grid_s[...], preferred_element_type=F32).astype(BF16)
-            for j in range(per_step):
-                send2[k * per_step + j] = block[j * 32 : (j + 1) * 32]
-            return carry
-
-        lax.fori_loop(0, devices // per_step, columns, 0)
-
-        def start2(i, carry):
-            copy2(i).start()
-            return carry
-
-        lax.fori_loop(1, devices, start2, 0)
-        recv2[me] = send2[me]
-
-    with jax.named_scope("row_table"):
-
-        def table_u(s, carry):
-            at = pl.ds(pl.multiple_of(s * TILE, TILE), TILE)
-            c1, s1 = e1c[pl.ds(s, 1), :], e1s[pl.ds(s, 1), :]
-            c2, s2 = e2c[...], e2s[...]
-            tab_s[at, :L_OUT] = (c1 * c2 - s1 * s2).astype(BF16)
-            tab_s[at, L_OUT:] = (s1 * c2 + c1 * s2).astype(BF16)
-            return carry
-
-        lax.fori_loop(0, devices, table_u, 0)
-
-    with jax.named_scope("screen"):
+            for j in range(devices // 4):
+                send2[start + j] = block[j * 32 : (j + 1) * 32]
+            return first
+
+        lax.fori_loop(0, 2, columns, (1 - core) * half)
+        swap.start()
+        lax.fori_loop(0, 2, columns, core * half)
+        swap.wait_recv()
+
+    with jax.named_scope("rows"):
         scale = 1.0 / math.sqrt(per_device * devices)
-        y = pixel(iota((M_DEV, L_OUT), 0) * devices + me, m_step).astype(F32) * (1.0 / G)
-        x = pixel(iota((M_DEV, L_OUT), 1), l_step).astype(F32) * (1.0 / G)
-        q = x * x + y * y
-        lowered = q / (1.0 + jnp.sqrt(1.0 - q))
-        for p in range(W):
-            turns = lowered * -w_ref[p]
-            turns = turns - jnp.floor(turns + 0.5)
-            scr_c[p] = cos_turns(turns) * scale
-            scr_s[p] = sin_turns(turns) * scale
-
-    def wait2(i, carry):
-        arrive2(i).wait_recv()
+
+        def summand(there):
+            for p in range(W):
+                at = slice(p * TILE, (p + 1) * TILE)
+                a_s[p * 32 : (p + 1) * 32, :TILE] = send2[core * half + there, :, at]
+                a_s[p * 32 : (p + 1) * 32, TILE : 2 * TILE] = recv2[there, :, at]
+
+            def image(k, carry):
+                at = pl.ds(pl.multiple_of(k * 256, 256), 256)
+                also = pl.ds(pl.multiple_of(k * 256 + L_OUT, 256), 256)
+                left = a_s[: 32 * W, : 2 * TILE]
+                by_cos = jnp.dot(left, tab_s[:, at], preferred_element_type=F32)
+                by_sin = jnp.dot(left, tab_s[:, also], preferred_element_type=F32)
+                total = jnp.zeros((M_DEV, 256), F32)
+                for p in range(W):
+                    r0, r1, r2 = p * 32, p * 32 + 16, p * 32 + 32
+                    real = by_cos[r0:r1] - by_sin[r1:r2]
+                    imag = by_sin[r0:r1] + by_cos[r1:r2]
+                    total = total + scr_c[there, p, :, at] * real - scr_s[there, p, :, at] * imag
+                own_s[:, at] = total * scale
+                return carry
+
+            lax.fori_loop(0, L_OUT // 256, image, 0, unroll=True)
+
+        def send_summand(i, carry):
+            there = lax.rem(chip + i, half)
+            summand(there)
+            send3[there] = own_s[...].astype(BF16)
+            copy3(i).start()
+            return carry
+
+        lax.fori_loop(1, half, send_summand, 0)
+        summand(chip)
+
+        def add(i, carry):
+            arrive3(i).wait_recv()
+            own_s[...] += recv3[lax.rem(chip - i + half, half)].astype(F32)
+            return carry
+
+        lax.fori_loop(1, half, add, 0)
+        out_ref[...] = own_s[...]
+
+    def drain1(i, carry):
+        copy1(i).wait_send()
         return carry
 
-    lax.fori_loop(1, devices, wait2, 0)
-
-    with jax.named_scope("rows"):
-
-        depth = min(TILE * devices, b_s.shape[1])
-        turns_k = TILE * devices // depth
-        for h in range(turns_k):
-
-            def regroup(s, carry):
-                at = pl.ds(pl.multiple_of(s * TILE, TILE), TILE)
-                for p in range(W):
-                    first = h * 32 * W + p * 32
-                    b_s[first : first + 32, at] = recv2[s + h * (depth // TILE), :, p * TILE : (p + 1) * TILE]
-                return carry
-
-            lax.fori_loop(0, depth // TILE, regroup, 0)
-
-        def rows_by(at):
-            total = None
-            for h in range(turns_k):
-                left = b_s[h * 32 * W : (h + 1) * 32 * W, :depth]
-                right = tab_s[h * depth : (h + 1) * depth, at]
-                part = jnp.dot(left, right, preferred_element_type=F32)
-                total = part if total is None else total + part
-            return total
-
-        def image(k, carry):
-            at = pl.ds(pl.multiple_of(k * 256, 256), 256)
-            also = pl.ds(pl.multiple_of(k * 256 + L_OUT, 256), 256)
-            by_cos = rows_by(at)
-            by_sin = rows_by(also)
-            total = jnp.zeros((M_DEV, 256), F32)
-            for p in range(W):
-                r0, r1, r2 = p * 32, p * 32 + 16, p * 32 + 32
-                real = by_cos[r0:r1] - by_sin[r1:r2]
-                imag = by_sin[r0:r1] + by_cos[r1:r2]
-                total = total + scr_c[p, :, at] * real - scr_s[p, :, at] * imag
-            out_ref[:, at] = total
-            return carry
-
-        lax.fori_loop(0, L_OUT // 256, image, 0)
-
-    def drain(i, carry):
-        copy1(i).wait_send()
-        copy2(i).wait_send()
+    def drain3(i, carry):
+        copy3(i).wait_send()
         return carry
 
-    lax.fori_loop(1, devices, drain, 0)
+    lax.fori_loop(1, devices, drain1, 0)
+    lax.fori_loop(1, half, drain3, 0)
+    swap.wait_send()
 
 
 def on_device(vis_values, tile_row, tile_col, row_offset, col_offset, plane, plane_w):
@@ -316,21 +317,22 @@
             pltpu.VMEM((2 * V_WIN, W * TILE), BF16),
             pltpu.VMEM((2 * M_DEV * devices, 2 * V_WIN), BF16),
             pltpu.VMEM((devices, 2 * M_DEV, W * TILE), BF16),
-            pltpu.VMEM((devices, 2 * M_DEV, W * TILE), BF16),
-            pltpu.VMEM((TILE * devices, 2 * L_OUT), BF16),
-            pltpu.VMEM((devices, L_OUT), F32),
-            pltpu.VMEM((devices, L_OUT), F32),
-            pltpu.VMEM((TILE, L_OUT), F32),
-            pltpu.VMEM((TILE, L_OUT), F32),
-            pltpu.VMEM((W, M_DEV, L_OUT), F32),
-            pltpu.VMEM((W, M_DEV, L_OUT), F32),
+            pltpu.VMEM((devices // 2, 2 * M_DEV, W * TILE), BF16),
+            pltpu.VMEM((2 * TILE, 2 * L_OUT), BF16),
+            pltpu.VMEM((devices // 2, W, M_DEV, L_OUT), F32),
+            pltpu.VMEM((devices // 2, W, M_DEV, L_OUT), F32),
+            pltpu.VMEM((M_DEV, L_OUT), F32),
+            pltpu.VMEM((devices // 2, M_DEV, L_OUT), BF16),
+            pltpu.VMEM((devices // 2, M_DEV, L_OUT), BF16),
             pltpu.SemaphoreType.DMA((devices,)),
             pltpu.SemaphoreType.DMA((devices,)),
-            pltpu.SemaphoreType.DMA((devices,)),
-            pltpu.SemaphoreType.DMA((devices,)),
+            pltpu.SemaphoreType.DMA,
+            pltpu.SemaphoreType.DMA,
+            pltpu.SemaphoreType.DMA((devices // 2,)),
+            pltpu.SemaphoreType.DMA((devices // 2,)),
         ],
         compiler_params=pltpu.CompilerParams(
-            collective_id=0, has_side_effects=True, vmem_limit_bytes=(32 if devices <= 16 else 62) * 2**20
+            collective_id=0, has_side_effects=True, vmem_limit_bytes=(40 if devices <= 16 else 62) * 2**20
         ),
     )(data, plane_w)
 

time: 51.6 us -> 39.4 us (0.76)
  Pallas kernels: 47.8 us -> 35.4 us
    pallas_call x1, Pallas kernels: 47.8 us -> 35.4 us  [on_device(): pl.pallas_call(functools.partial(kernel, devices, cap, group, width, per_...]
where the time goes in v1:
time: 39.4 us; the launch traced here: 38.9 us
  Pallas kernels  35.4 us (90%)
  local copies, waits for them, and re-layouts  3.39 us (9%)
    pallas_call x1, Pallas kernels, on_device(): pl.pallas_call(functools.partial(kernel, devices, cap, group, width, per_...  35.4 us
    unnamed x15, local copies, waits for them, and re-layouts  3.34 us

profile of v1, /device:TPU:13, one launch (start us, length us, event | category | flops | bytes accessed | tf_op | source)
XLA Modules:
  0.0 38.9 jit_solution(16651936162360376071)
XLA Ops:
  0.0 0.0 copy-start.6
  0.0 0.7 %copy-done.6 = s32[1024]{0:T(1024)S(1)} copy-done((s32[1024]{0:T(1024)S(1)}, s32[1024]{0:T(1024)}, u32[]{:S(2)}) %copy-start.6) | copy-done | bytes 4120
  0.7 0.0 copy-start.5
  0.7 0.7 %copy-done.5 = bf16[2,1024]{1,0:T(2,128)(2,1)S(1)} copy-done((bf16[2,1024]{1,0:T(2,128)(2,1)S(1)}, bf16[2,1024]{1,0:T(2,128)(2,1)}, u32[]{:S(2)}) %copy-start.5) | copy-done | bytes 4120
  1.4 0.0 copy-start.2
  1.4 0.0 copy-start.3
  1.4 0.0 copy-start.4
  1.4 0.0 copy-start.1
  1.4 0.6 %copy-done.2 = s32[1024]{0:T(1024)S(1)} copy-done((s32[1024]{0:T(1024)S(1)}, s32[1024]{0:T(1024)}, u32[]{:S(2)}) %copy-start.2) | copy-done | bytes 4120
  2.1 0.0 copy-done.3
  2.1 0.0 copy-done.4
  2.1 0.0 copy-done.1
  2.2 0.0 copy-start
  2.2 0.6 %copy-done = f32[8]{0:T(128)S(1)} copy-done((f32[8]{0:T(128)S(1)}, f32[8]{0:T(128)}, u32[]{:S(2)}) %copy-start) | copy-done | bytes 56
  2.8 35.4 %shard_map.73 = f32[16,1024]{1,0:T(8,128)S(1)} custom-call(f32[8,1024]{1,0:T(8,128)S(1)} %pad_maximum_fusion.data_ref, f32[8]{0:T(128)S(1)} %copy-done), custom_call_target="tpu_custom_call" | custom-call | tf_op jit(solution)/shard_map/pallas_call | solution.py:306
  38.3 0.6 %copy.9 = f32[16,1024]{1,0:T(8,128)} copy(f32[16,1024]{1,0:T(8,128)S(1)} %shard_map.73) | data formatting | bytes 131072
  (6 shorter events, 0.1 us)
Async XLA Ops:
  0.0 0.7 %copy-start.6 = (s32[1024]{0:T(1024)S(1)}, s32[1024]{0:T(1024)}, u32[]{:S(2)}) copy-start(s32[1024]{0:T(1024)} %param.12) | copy-start | bytes 12292
  0.7 0.7 %copy-start.5 = (bf16[2,1024]{1,0:T(2,128)(2,1)S(1)}, bf16[2,1024]{1,0:T(2,128)(2,1)}, u32[]{:S(2)}) copy-start(bf16[2,1024]{1,0:T(2,128)(2,1)} %param.7) | copy-start | bytes 12292
  1.4 0.7 %copy-start.2 = (s32[1024]{0:T(1024)S(1)}, s32[1024]{0:T(1024)}, u32[]{:S(2)}) copy-start(s32[1024]{0:T(1024)} %param.9) | copy-start | bytes 12292
  1.4 0.7 %copy-start.3 = (s32[1024]{0:T(1024)S(1)}, s32[1024]{0:T(1024)}, u32[]{:S(2)}) copy-start(s32[1024]{0:T(1024)} %param.11) | copy-start | bytes 12292
  1.4 0.7 %copy-start.4 = (s32[1024]{0:T(1024)S(1)}, s32[1024]{0:T(1024)}, u32[]{:S(2)}) copy-start(s32[1024]{0:T(1024)} %param.8) | copy-start | bytes 12292
  1.4 0.7 %copy-start.1 = (s32[1024]{0:T(1024)S(1)}, s32[1024]{0:T(1024)}, u32[]{:S(2)}) copy-start(s32[1024]{0:T(1024)} %param.10) | copy-start | bytes 12292
  2.2 0.7 %copy-start = (f32[8]{0:T(128)S(1)}, f32[8]{0:T(128)}, u32[]{:S(2)}) copy-start(f32[8]{0:T(128)} %w_ref.1) | copy-start | bytes 100

commit v2 on v1

--- a/solution.py
+++ b/solution.py
@@ -57,9 +57,9 @@
 
 def kernel(
     devices, cap, group, width, per_device,
-    data_ref, w_ref, out_ref,
-    key_s, send1, recv1, a_s, b_s, grid_s, tv_s, send2, recv2, tab_s, scr_c, scr_s, own_s, send3, recv3,
-    ss1, rs1, ss2, rs2, ss3, rs3,
+    vis_ref, plane_ref, row_ref, tcol_ref, col_ref, trow_ref, w_ref, out_ref,
+    ints_s, data_s, key_s, send1, recv1, a_s, b_s, grid_s, tv_s, send2, recv2, tab_s, scr_c, scr_s, own_s, send3, recv3,
+    ss1, rs1, ss2, rs2, ss3, rs3, in_sem,
 ):
     me = lax.axis_index("row")
     blocks = devices // group
@@ -74,7 +74,13 @@
         )
         return carry
 
+    inputs = (plane_ref, row_ref, tcol_ref, col_ref, trow_ref)
+    fetches = [pltpu.make_async_copy(ref, ints_s.at[k], in_sem.at[k]) for k, ref in enumerate(inputs)]
+    for fetch in fetches:
+        fetch.start()
     lax.fori_loop(1, devices, greet, 0)
+    for fetch in fetches:
+        fetch.wait()
 
     def copy1(i):
         peer = lax.rem(me + i, devices)
@@ -114,7 +120,16 @@
         )
 
     with jax.named_scope("pack"):
-        data = data_ref[...]
+        data_s[0:2, :] = vis_ref[...].astype(F32)
+        for c in range(per_device // 128):
+            at = slice(c * 128, (c + 1) * 128)
+            data_s[2:3, at] = ints_s[0, c : c + 1, :].astype(F32) + 1.0
+            data_s[3:4, at] = ints_s[1, c : c + 1, :].astype(F32)
+            data_s[4:5, at] = ints_s[2, c : c + 1, :].astype(F32)
+            data_s[5:6, at] = ints_s[3, c : c + 1, :].astype(F32)
+            data_s[6:7, at] = ints_s[4, c : c + 1, :].astype(F32)
+        data_s[7:8, :] = jnp.zeros((1, per_device), F32)
+        data = data_s[...]
         member = jnp.where(data[6:7, :] == iota((devices, per_device), 0).astype(F32), 1.0, 0.0)
         parts = [member[:, c * 128 : (c + 1) * 128] for c in range(per_device // 128)]
         below = jnp.where(iota((128, 128), 0) < iota((128, 128), 1), 1.0, 0.0).astype(BF16)
@@ -129,17 +144,25 @@
         def packed(d):
             slot = iota((width, per_device), 0).astype(F32)
             hot = jnp.where(slot == key_s[pl.ds(d, 1), :], 1.0, 0.0).astype(BF16)
-            return lax.dot_general(low, hot, NT, preferred_element_type=F32)
+            found = lax.dot_general(low, hot, NT, preferred_element_type=F32)
+            second = found[:, 128:] if width > 128 else jnp.zeros((8, 128), F32)
+            return jnp.concatenate([found[:, :128], second], axis=0).astype(BF16)
 
         pl.semaphore_wait(barrier, devices - 1)
 
-        def send_block(i, carry):
-            d = lax.rem(me + i, devices)
-            send1[d] = packed(d)
-            copy1(i).start()
-            return carry
-
-        lax.fori_loop(1, devices, send_block, 0)
+        batch = 3 if (devices - 1) % 3 == 0 else 1
+
+        def send_block(k, carry):
+            steps = [k * batch + 1 + j for j in range(batch)]
+            peers = [lax.rem(me + i, devices) for i in steps]
+            found = [packed(d) for d in peers]
+            for d, block in zip(peers, found):
+                send1[d] = block
+            for i in steps:
+                copy1(i).start()
+            return carry
+
+        lax.fori_loop(0, (devices - 1) // batch, send_block, 0)
         recv1[me] = packed(me)
 
     with jax.named_scope("tables"):
@@ -192,9 +215,10 @@
     with jax.named_scope("spread"):
 
         def spread(k, carry):
-            block = recv1[k * group]
+            block = recv1[k * group].astype(F32)
             for j in range(1, group):
-                block = block + recv1[k * group + j]
+                block = block + recv1[k * group + j].astype(F32)
+            block = jnp.concatenate([block[:8], block[8:]], axis=1)[:, :width]
             at = pl.ds(pl.multiple_of(k * width, width), width)
             down = iota((TILE, width), 0).astype(F32)
             rows_k = taper(down - block[3:4, :]).astype(BF16)
@@ -209,7 +233,7 @@
                     a_s[first : first + TILE, at] = (cols_k * value).astype(BF16)
             return carry
 
-        lax.fori_loop(0, blocks, spread, 0)
+        lax.fori_loop(0, blocks, spread, 0, unroll=2)
 
     with jax.named_scope("gridding"):
 
@@ -300,18 +324,19 @@
     group = max(1, 128 // cap)
     width = cap * group
     slots = width * (devices // group)
-    ints = jnp.stack([plane + 1, row_offset, tile_col, col_offset, tile_row, jnp.zeros_like(plane)])
-    data = jnp.concatenate([vis_values.astype(F32), ints.astype(F32)], axis=0)
+    ints = [x.reshape(per_device // 128, 128) for x in (plane, row_offset, tile_col, col_offset, tile_row)]
     vmem = pl.BlockSpec(memory_space=pltpu.VMEM)
     return pl.pallas_call(
         functools.partial(kernel, devices, cap, group, width, per_device),
         out_shape=jax.ShapeDtypeStruct((M_DEV, L_OUT), F32),
-        in_specs=[vmem, pl.BlockSpec(memory_space=pltpu.SMEM)],
+        in_specs=[vmem] + [pl.BlockSpec(memory_space=pltpu.HBM)] * 5 + [pl.BlockSpec(memory_space=pltpu.SMEM)],
         out_specs=vmem,
         scratch_shapes=[
+            pltpu.VMEM((5, per_device // 128, 128), I32),
+            pltpu.VMEM((8, per_device), F32),
             pltpu.VMEM((devices, per_device), F32),
-            pltpu.VMEM((devices, 8, width), F32),
-            pltpu.VMEM((devices, 8, width), F32),
+            pltpu.VMEM((devices, 16, 128), BF16),
+            pltpu.VMEM((devices, 16, 128), BF16),
             pltpu.VMEM((2 * V_WIN, slots), BF16),
             pltpu.VMEM((W * TILE, slots), BF16),
             pltpu.VMEM((2 * V_WIN, W * TILE), BF16),
@@ -330,11 +355,12 @@
             pltpu.SemaphoreType.DMA,
             pltpu.SemaphoreType.DMA((devices // 2,)),
             pltpu.SemaphoreType.DMA((devices // 2,)),
+            pltpu.SemaphoreType.DMA((5,)),
         ],
         compiler_params=pltpu.CompilerParams(
-            collective_id=0, has_side_effects=True, vmem_limit_bytes=(40 if devices <= 16 else 62) * 2**20
+            collective_id=0, has_side_effects=True, vmem_limit_bytes=64 * 2**20
         ),
-    )(data, plane_w)
+    )(vis_values, *ints, plane_w)
 
 
 def solution(mesh):

time: 39.4 us -> 37.6 us (0.954)
  local copies, waits for them, and re-layouts: 3.39 us -> 1.47 us
    unnamed x15 -> x1, local copies, waits for them, and re-layouts: 3.34 us -> 1.47 us
where the time goes in v2:
time: 37.6 us; the launch traced here: 37.1 us
  Pallas kernels  35.6 us (95%)
  local copies, waits for them, and re-layouts  1.47 us (4%)
    pallas_call x1, Pallas kernels, on_device(): pl.pallas_call(functools.partial(kernel, devices, cap, group, width, per_...  35.6 us
    unnamed x1, local copies, waits for them, and re-layouts  1.47 us

profile of v2, /device:TPU:13, one launch (start us, length us, event | category | flops | bytes accessed | tf_op | source)
XLA Modules:
  0.0 37.1 jit_solution(1687654239857004983)
XLA Ops:
  0.0 35.6 %shard_map.73 = f32[16,1024]{1,0:T(8,128)} custom-call(bf16[2,1024]{1,0:T(2,128)(2,1)} %vis_ref.1, s32[8,128]{1,0:T(8,128)} %bitcast.5, s32[8,128]{1,0:T(8,128)} %bitcast.6, s32[8,128]{1,0:T(8,128)} %bitcast.7, s32[8,128]{1,0:T(8,128)} %bitcast.8, s32[8,128]{1,0:T(8,128)} %bitcast.9, f32[8]{0:T(128)} %w_ref.1), custom_call_target="tpu_custom_call" | custom-call | tf_op jit(solution)/shard_map/pallas_call | solution.py:329
  35.6 1.5 %copy.9 = f32[16,1024]{1,0:T(8,128)} copy(f32[16,1024]{1,0:T(8,128)} %shard_map.73) | data formatting | bytes 131072

commit v3 on v2

--- a/solution.py
+++ b/solution.py
@@ -204,7 +204,8 @@
                 scr_s[there, p] = sin_turns(turns)
             return carry
 
-        lax.fori_loop(0, half, screen, 0)
+        early = half - half // 4
+        lax.fori_loop(0, early, screen, 0)
 
     def wait1(i, carry):
         arrive1(i).wait_recv()
@@ -258,6 +259,7 @@
         lax.fori_loop(0, 2, columns, (1 - core) * half)
         swap.start()
         lax.fori_loop(0, 2, columns, core * half)
+        lax.fori_loop(early, half, screen, 0)
         swap.wait_recv()
 
     with jax.named_scope("rows"):

time: 37.6 us -> 36.6 us (0.973)
  Pallas kernels: 35.6 us -> 34.5 us
    pallas_call x1, Pallas kernels: 35.6 us -> 34.5 us  [on_device(): pl.pallas_call(functools.partial(kernel, devices, cap, group, width, per_...]
where the time goes in v3:
time: 36.6 us; the launch traced here: 36 us
  Pallas kernels  34.5 us (94%)
  local copies, waits for them, and re-layouts  1.47 us (4%)
    pallas_call x1, Pallas kernels, on_device(): pl.pallas_call(functools.partial(kernel, devices, cap, group, width, per_...  34.5 us
    unnamed x1, local copies, waits for them, and re-layouts  1.47 us

profile of v3, /device:TPU:13, one launch (start us, length us, event | category | flops | bytes accessed | tf_op | source)
XLA Modules:
  0.0 36.0 jit_solution(16510305470061396503)
XLA Ops:
  0.0 34.5 %shard_map.73 = f32[16,1024]{1,0:T(8,128)} custom-call(bf16[2,1024]{1,0:T(2,128)(2,1)} %vis_ref.1, s32[8,128]{1,0:T(8,128)} %bitcast.5, s32[8,128]{1,0:T(8,128)} %bitcast.6, s32[8,128]{1,0:T(8,128)} %bitcast.7, s32[8,128]{1,0:T(8,128)} %bitcast.8, s32[8,128]{1,0:T(8,128)} %bitcast.9, f32[8]{0:T(128)} %w_ref.1), custom_call_target="tpu_custom_call" | custom-call | tf_op jit(solution)/shard_map/pallas_call | solution.py:331
  34.5 1.5 %copy.9 = f32[16,1024]{1,0:T(8,128)} copy(f32[16,1024]{1,0:T(8,128)} %shard_map.73) | data formatting | bytes 131072
